TPU v7x, 32 devices: a whole 2x2x4 slice. The times are simulated.
32 devices in a mesh: grp: 2 (over core), aux: 4 (over y, x), orb: 4 (over z).
Axes of the slice: x: 2, y: 2, z: 4, core: 2. Of those that a mesh axis runs over, the one named last changes fastest.
Arguments:
- fitted_tensor: bfloat16 [4, 8192, 8192], P('grp', 'aux', 'orb'), may hold values from -0.23925781 to 0.23925781
- block_mask: int32 [2, 64, 64], P('grp'), may hold values 0 or 1
- orbitals: bfloat16 [8192, 256], P('aux'), may hold values from -0.0625 to 0.0625
- nuclear: float32 [8192], replicated, may hold values from 0.5 to 1.5
- centres: float32 [3, 8192], replicated, may hold values from 0 to 8
- mm_positions: float32 [3, 32768], P(None, ('grp', 'aux', 'orb')), may hold values from 0 to 8
- mm_charges: float32 [32768], P(('grp', 'aux', 'orb')), may hold values from -0.12 to 0.12
- neighbours: int32 [32, 2], P(('grp', 'aux', 'orb')), may hold values from 0 to 63, all different within a row
Outputs:
- fock: float32 [8192, 8192], P(('aux', 'orb'))
- mm_potential: float32 [32768], P(('grp', 'aux', 'orb'))
Inputs may be any that keep to these rules, and one draw needn't show every extreme that they name: `neighbours`: each row names 2 different blocks; every block is named by some row.
All inputs are finite; a program needn't handle non-finite values. No bound on the sum of `block_mask` on one device may be relied on, other than what follows from the above.
Results may differ from a plain program's by a relative error of at most 0.01.
Values may be sent and summed in bfloat16 or wider, within the bound.
A program may use at most 128 MiB of HBM per device.

v0:
```python
import jax
import jax.numpy as jnp
from jax import lax
from jax.sharding import PartitionSpec as P

BLK = 128
softening = 1.0


def near_kernel(picker, centre_blocks, charge_blocks, atom_xyz):
    near_xyz = jnp.einsum("kb,cbj->ckj", picker, centre_blocks, precision=lax.Precision.HIGHEST)
    near_xyz = near_xyz.reshape(3, picker.shape[0] * centre_blocks.shape[2])
    near_q = jnp.dot(picker, charge_blocks, precision=lax.Precision.HIGHEST).reshape(-1)
    offsets = near_xyz[:, :, None] - atom_xyz[:, None, :]
    kernel = lax.rsqrt(jnp.sum(offsets * offsets, axis=0) + softening)
    return (kernel, near_q)


def add_diagonal(fock_rows, first_row, field_vec):
    row_count = fock_rows.shape[0]
    values = lax.dynamic_slice_in_dim(field_vec, first_row, row_count, 0)
    row_ids = jnp.arange(row_count, dtype=jnp.int32)[:, None]
    col_ids = jnp.arange(fock_rows.shape[1], dtype=jnp.int32)[None, :]
    on_diagonal = col_ids == first_row + row_ids
    return fock_rows + jnp.where(on_diagonal, values[:, None], jnp.float32(0.0))


def block_picker(first, count, block_total):
    positions = (first + jnp.arange(count, dtype=jnp.int32)) // BLK
    block_ids = jnp.arange(block_total, dtype=jnp.int32)
    return (positions[:, None] == block_ids[None, :]).astype(jnp.float32)


def per_device(
    fitted_tensor, block_mask, orbitals, nuclear, centres, mm_positions, mm_charges, neighbours
):
    row_span = fitted_tensor.shape[1]
    col_span = fitted_tensor.shape[2]
    orb_count = lax.axis_size("orb")
    aux_id = lax.axis_index("aux")
    orb_id = lax.axis_index("orb")
    own_span = row_span // orb_count
    block_total = block_mask.shape[1]
    whole_c = lax.all_gather(orbitals, "aux", axis=0, tiled=True)
    row_start = aux_id * row_span
    col_start = orb_id * col_span
    window_c = lax.dynamic_slice_in_dim(whole_c, col_start, col_span, 0)
    row_pick = block_picker(row_start, row_span, block_total)
    col_pick = block_picker(col_start, col_span, block_total)
    row_bits = jnp.dot(row_pick, block_mask[0].astype(jnp.float32), precision=lax.Precision.HIGHEST)
    mask_wide = jnp.dot(row_bits, col_pick.T, precision=lax.Precision.HIGHEST).astype(jnp.bfloat16)
    masked = fitted_tensor * mask_wide[None]
    x_partial = jnp.einsum("pmn,ni->pmi", masked, window_c, preferred_element_type=jnp.float32)
    x_rows = lax.psum(x_partial, "orb")
    own_rows = lax.dynamic_slice_in_dim(x_rows, orb_id * own_span, own_span, 1)
    x_own = own_rows.astype(jnp.bfloat16)
    own_c = lax.dynamic_slice_in_dim(orbitals, orb_id * own_span, own_span, 0)
    dens_part = 2.0 * jnp.einsum("pmi,mi->p", x_own, own_c, preferred_element_type=jnp.float32)
    densities = lax.psum(dens_part, ("aux", "orb")).astype(jnp.bfloat16)
    coulomb_block = jnp.einsum("pmn,p->mn", masked, densities, preferred_element_type=jnp.float32)
    coulomb = lax.all_to_all(coulomb_block, "orb", split_axis=0, concat_axis=1, tiled=True)
    c_float = whole_c.astype(jnp.float32)
    population = 2.0 * jnp.sum(c_float * c_float, axis=1)
    qm_charge = nuclear - population
    centre_blocks = centres.reshape(3, block_total, BLK)
    charge_blocks = qm_charge.reshape(block_total, BLK)
    picker = (neighbours[0][:, None] == jnp.arange(block_total, dtype=jnp.int32)[None, :]).astype(
        jnp.float32
    )
    kernel, near_q = near_kernel(picker, centre_blocks, charge_blocks, mm_positions)
    mm_potential = jnp.dot(near_q, kernel, precision=lax.Precision.HIGHEST)
    contrib = jnp.dot(kernel, mm_charges, precision=lax.Precision.HIGHEST).reshape(
        picker.shape[0], BLK
    )
    field_part = jnp.dot(picker.T, contrib, precision=lax.Precision.HIGHEST)
    field_sum = lax.psum(field_part, ("grp", "aux", "orb"))
    field_vec = field_sum.reshape(-1)
    own_first = row_start + orb_id * own_span
    exchange_part = jnp.einsum(
        "pmi,pni->mn",
        x_own,
        lax.all_gather(x_own, ("aux", "orb"), axis=1, tiled=True),
        preferred_element_type=jnp.float32,
    )
    fock_part = coulomb - 0.5 * exchange_part
    fock_sum = lax.psum(fock_part, "grp")
    fock = add_diagonal(fock_sum, own_first, field_vec)
    return (fock, mm_potential)


def solution(mesh):
    in_specs = (
        P("grp", "aux", "orb"),
        P("grp", None, None),
        P("aux", None),
        P(),
        P(),
        P(None, ("grp", "aux", "orb")),
        P(("grp", "aux", "orb")),
        P(("grp", "aux", "orb"), None),
    )
    out_specs = (P(("aux", "orb"), None), P(("grp", "aux", "orb")))
    return jax.shard_map(
        per_device, mesh=mesh, in_specs=in_specs, out_specs=out_specs, check_vma=False
    )
```

profile of v0, /device:TPU:0, one launch (start us, length us, event | category | flops | bytes accessed | tf_op | source)
XLA Modules:
  0.0 848.3 jit_solution(9946186388667584154)
XLA Ops:
  7.2 0.0 all-gather.3.cloned.1.call-start
  7.2 0.7 all-gather.3.cloned.1.call-update
  8.0 1.0 bitcast_convert_fusion
  9.0 1.7 fusion.6
  10.6 7.5 convolution_convert_fusion
  18.1 14.8 %broadcast_multiply_fusion = bf16[2,2048,2048]{2,1,0:T(8,128)(2,1)} fusion(bf16[2,2048,2048]{2,1,0:T(8,128)(2,1)} %param.8, bf16[2048,2048]{1,0:T(8,128)(2,1)S(1)} %convolution_convert_fusion), kind=kLoop, calls=%fused_computation.7 | loop fusion | flops 8388608 | bytes 41943040 | tf_op jit(solution)/shard_map/mul | solution.py:52
  32.9 32.4 %all-gather.3.cloned.1.call-done = bf16[8192,256]{1,0:T(8,128)(2,1)} async-done(((bf16[2048,256]{1,0:T(8,128)(2,1)}), bf16[8192,256]{1,0:T(8,128)(2,1)}) %all-gather.3.cloned.1.call-update) | async-done | bytes 4194320 | tf_op jit(solution)/shard_map/all_gather | solution.py:44
  65.3 12.5 %fusion.3 = f32[2,2048,256]{2,1,0:T(8,128)} fusion(bf16[2,2048,2048]{2,1,0:T(8,128)(2,1)} %broadcast_multiply_fusion, bf16[8192,256]{1,0:T(8,128)(2,1)} %all-gather.3.cloned.1.call-done, s32[]{:T(128)S(6)} %select_n.32), kind=kOutput, calls=%fused_computation.12 | convolution fusion | flops 4294967296 | bytes 22020100 | tf_op jit(solution)/shard_map/pmn,ni->pmi/dot_general | solution.py:53
  77.8 147.1 %all-reduce.4 = bf16[2,2048,256]{2,1,0:T(8,128)(2,1)S(1)} all-reduce(f32[2,2048,256]{2,1,0:T(8,128)} %fusion.3), channel_id=1, replica_groups=mesh['grp'=2,'aux'=4,'orb'=4] {'orb'}, use_global_device_ids=true, to_apply=%region_0.1 | all-reduce | flops 1048576 | bytes 6291456 | tf_op jit(solution)/shard_map/psum | solution.py:54
  224.9 1.0 multiply_reduce_fusion.2
  225.9 38.2 %psum.29 = bf16[2]{0:T(256)(128)(2,1)S(1)} all-reduce(f32[2]{0:T(128)S(1)} %broadcast_multiply_fusion.1), channel_id=1, replica_groups=mesh['grp'=2,'aux'=4,'orb'=4] {'aux','orb'}, use_global_device_ids=true, to_apply=%region_1.2 | all-reduce | flops 2 | bytes 12 | tf_op jit(solution)/shard_map/psum | solution.py:59
  264.2 28.8 %fusion.1 = f32[1,2048,2048]{2,0,1:T(1,128)S(1)} fusion(bf16[2,2048,2048]{2,1,0:T(8,128)(2,1)} %broadcast_multiply_fusion, bf16[2]{0:T(256)(128)(2,1)S(1)} %psum.29), kind=kOutput, calls=%fused_computation.4 | convolution fusion | flops 16777216 | bytes 33554436 | tf_op jit(solution)/shard_map/pmn,p->mn/dot_general | solution.py:60
  292.9 11.3 %copy.18 = f32[1,2048,2048]{2,1,0:T(8,128)} copy(f32[1,2048,2048]{2,0,1:T(1,128)S(1)} %fusion.1) | data formatting | bytes 33554432 | tf_op jit(solution)/shard_map/pmn,p->mn/dot_general | solution.py:60
  304.2 7.0 all-to-all-start
  311.2 0.0 all-gather.5.cloned.1.call-start
  311.2 0.7 all-gather.5.cloned.1.call-update
  312.0 0.0 all-reduce.3.cloned.1.call-start
  312.0 433.2 %all-to-all-done = f32[4,512,2048]{2,1,0:T(8,128)} async-done(((f32[4,512,2048]{2,1,0:T(8,128)}), f32[4,512,2048]{2,1,0:T(8,128)}, u32[]{:S(2)}, u32[]{:S(2)}) %all-to-all-start) | async-done | bytes 16777248 | tf_op jit(solution)/shard_map/all_to_all | solution.py:61
  745.2 11.9 %copy.21 = f32[4,64,8,2048]{3,2,0,1:T(8,128)} copy(f32[4,64,8,2048]{3,2,1,0:T(8,128)} %bitcast.23) | data formatting | bytes 33554432 | tf_op jit(solution)/shard_map/all_to_all | solution.py:61
  757.0 14.4 %fusion = f32[512,8192]{1,0:T(8,128)} fusion(f32[512,8192]{1,0:T(8,128)} %bitcast.59, bf16[2,512,256]{2,1,0:T(8,128)(2,1)S(1)} %copy-done.1, bf16[2,8192,256]{2,1,0:T(8,128)(2,1)} %all-gather.5.cloned.1.call-done), kind=kOutput, calls=%fused_computation.1 | convolution fusion | flops 4303355904 | bytes 42467328 | tf_op jit(solution)/shard_map/pmi,pni->mn/dot_general | solution.py:79
  771.5 0.9 copy-done.2
  772.3 0.2 convolution_bitcast_fusion.1
  772.5 0.4 multiply_reduce_fusion.1
  772.9 1.0 fusion.8
  773.9 0.3 convolution_bitcast_fusion
  774.2 37.3 %psum.31 = f32[8192]{0:T(1024)S(1)} all-reduce(f32[8192]{0:T(1024)S(1)} %convolution_bitcast_fusion), channel_id=1, replica_groups=mesh['grp'=2,'aux'=4,'orb'=4] {'grp','aux','orb'}, use_global_device_ids=true, to_apply=%region_4.5 | all-reduce | flops 8192 | bytes 65536 | tf_op jit(solution)/shard_map/psum | solution.py:76
  811.5 0.1 dynamic_slice.15
  811.6 3.8 multiply_reduce_fusion
  815.3 0.2 fusion.15
  815.5 1.3 fusion.7
  816.8 12.9 %all-reduce.3.cloned.1.call-done = f32[512,8192]{1,0:T(8,128)} async-done(((f32[512,8192]{1,0:T(8,128)}), f32[512,8192]{1,0:T(8,128)}) %all-reduce.3.cloned.1.call-update) | async-done | bytes 16777232 | tf_op jit(solution)/shard_map/psum | solution.py:86
  829.7 12.1 %select_add_fusion = f32[512,8192]{1,0:T(8,128)} fusion(f32[512,8192]{1,0:T(8,128)} %all-reduce.3.cloned.1.call-done, f32[512]{0:T(512)S(1)} %dynamic_slice.15, s32[512]{0:T(512)S(1)} %iota_add_fusion.2), kind=kLoop, calls=%fused_computation.2 | loop fusion | flops 12582912 | bytes 33558528 | tf_op jit(solution)/shard_map/add | solution.py:25
  (18 shorter events, 0.1 us)
Async XLA Ops:
  7.2 765.8 %copy-start = (f32[1024]{0:T(1024)S(1)}, f32[1024]{0:T(1024)}, u32[]{:S(2)}) copy-start(f32[1024]{0:T(1024)} %param.14) | copy-start | bytes 12292
  7.2 58.1 %all-gather.3.cloned.1.call-start = ((), (), s32[]{:S(2)}) async-start(), calls=%async_computation.1 | async-start | bytes 5242880 | tf_op jit(solution)/shard_map/all_gather | solution.py:44
  304.2 440.9 %all-to-all-start = ((f32[4,512,2048]{2,1,0:T(8,128)}), f32[4,512,2048]{2,1,0:T(8,128)}, u32[]{:S(2)}, u32[]{:S(2)}) async-start(f32[4,512,2048]{2,1,0:T(8,128)} %bitcast.58), calls=%async_computation | async-start | bytes 33554432 | tf_op jit(solution)/shard_map/all_to_all | solution.py:61
  311.2 445.8 %all-gather.5.cloned.1.call-start = ((), (), s32[]{:S(2)}) async-start(), calls=%async_computation.2 | async-start | bytes 8912896 | tf_op jit(solution)/shard_map/all_gather | solution.py:82
  312.0 517.8 %all-reduce.3.cloned.1.call-start = ((), (), s32[]{:S(2)}) async-start(), calls=%async_computation.3 | async-start | bytes 33554432 | tf_op jit(solution)/shard_map/psum | solution.py:86
  745.2 11.9 %copy-start.1 = (bf16[2,512,256]{2,1,0:T(8,128)(2,1)S(1)}, bf16[2,512,256]{2,1,0:T(8,128)(2,1)}, u32[]{:S(2)}) copy-start(bf16[2,512,256]{2,1,0:T(8,128)(2,1)} %get-tuple-element.3) | copy-start | bytes 1572868
  771.4 0.9 copy-start.2
  771.4 0.9 copy-start.5
  771.4 1.1 copy-start.4
  771.4 43.9 %copy-start.3 = (f32[8192]{0:T(1024)S(1)}, f32[8192]{0:T(1024)}, u32[]{:S(2)}) copy-start(f32[8192]{0:T(1024)} %param.11) | copy-start | bytes 98308
Sparse Core Ops, SparseCore 0:
  9.9 55.3 all-gather.2
  314.8 381.6 all-gather.4
  771.6 58.0 all-reduce.2
where the time goes:
time: 849 us; the launch traced here: 848 us
  waiting for transfers between devices  480 us (57%)
  blocking collectives  223 us (26%)
  matrix products  67.7 us (8%)
  other arithmetic  33.1 us (4%)
  local copies, waits for them, and re-layouts  24.2 us (3%)
  between operations  13.9 us (2%)
    all_to_all x1, waiting for transfers between devices, per_device(): lax.all_to_all(coulomb_block, 'orb', split_axis=0, concat_axis=1, tiled=T...  433 us
    psum x1, blocking collectives, per_device(): x_rows = lax.psum(x_partial, 'orb')  147 us
    psum x1, blocking collectives, per_device(): densities = lax.psum(dens_part, ('aux', 'orb')).astype(jnp.bfloat16)  38.2 us
    psum x1, blocking collectives, per_device(): field_sum = lax.psum(field_part, ('grp', 'aux', 'orb'))  37.3 us
    all_gather x1, waiting for transfers between devices, per_device(): whole_c = lax.all_gather(orbitals, 'aux', axis=0, tiled=True)  32.4 us
    dot_general x1, matrix products, per_device(): jnp.einsum('pmn,p->mn', masked, densities, preferred_element_type=jnp.flo...  28.8 us
  transfers between devices with their start and end apart: 4, of which 3 were waited for; matrix products, arithmetic and copies ran while one was open for 5% of the time, Pallas kernels for 0%

commit v1 on v0

--- a/solution.py
+++ b/solution.py
@@ -73,7 +73,7 @@
         picker.shape[0], BLK
     )
     field_part = jnp.dot(picker.T, contrib, precision=lax.Precision.HIGHEST)
-    field_sum = lax.psum(field_part, ("grp", "aux", "orb"))
+    field_sum = lax.psum(lax.psum(field_part, ("aux", "orb")), "grp")
     field_vec = field_sum.reshape(-1)
     own_first = row_start + orb_id * own_span
     exchange_part = jnp.einsum(

time: 849 us -> 878 us (1.034)
  waiting for transfers between devices: 480 us -> 505 us
    psum x1, waiting for transfers between devices: 12.9 us -> 49.1 us  [per_device(): fock_sum = lax.psum(fock_part, 'grp')]
    psum x1, blocking collectives: 38.2 us -> 73.3 us  [per_device(): densities = lax.psum(dens_part, ('aux', 'orb')).astype(jnp.bfloat16)]
    psum x1, blocking collectives: 37.3 us -> 3.41 us  [per_device(): field_sum = lax.psum(lax.psum(field_part, ('aux', 'orb')), 'grp')]
where the time goes in v1:
time: 878 us
  waiting for transfers between devices  505 us (58%)
  blocking collectives  224 us (26%)
  matrix products  69.3 us (8%)
  other arithmetic  34.7 us (4%)
  local copies, waits for them, and re-layouts  23.3 us (3%)
  between operations  13.9 us (2%)
    all_to_all x1, waiting for transfers between devices, per_device(): lax.all_to_all(coulomb_block, 'orb', split_axis=0, concat_axis=1, tiled=T...  426 us
    psum x1, blocking collectives, per_device(): x_rows = lax.psum(x_partial, 'orb')  147 us
    psum x1, blocking collectives, per_device(): densities = lax.psum(dens_part, ('aux', 'orb')).astype(jnp.bfloat16)  73.3 us
    psum x1, waiting for transfers between devices, per_device(): fock_sum = lax.psum(fock_part, 'grp')  49.1 us
    dot_general x1, matrix products, per_device(): jnp.einsum('pmn,p->mn', masked, densities, preferred_element_type=jnp.flo...  28.8 us
    all_gather x1, waiting for transfers between devices, per_device(): whole_c = lax.all_gather(orbitals, 'aux', axis=0, tiled=True)  28.5 us
  transfers between devices with their start and end apart: 4, of which 3 were waited for; matrix products, arithmetic and copies ran while one was open for 5% of the time, Pallas kernels for 0%

profile of v1, /device:TPU:0, one launch (start us, length us, event | category | flops | bytes accessed | tf_op | source)
XLA Modules:
  0.0 877.6 jit_solution(1306730533184363830)
XLA Ops:
  7.2 0.0 all-gather.3.cloned.1.call-start
  7.2 0.7 all-gather.3.cloned.1.call-update
  7.9 1.1 convolution_bitcast_fusion
  9.1 1.0 bitcast_convert_fusion
  10.1 1.2 multiply_reduce_fusion.1
  11.3 1.0 fusion.8
  12.2 1.0 fusion.29
  13.2 1.7 fusion.6
  14.9 7.5 convolution_convert_fusion
  22.4 14.4 %broadcast_multiply_fusion = bf16[2,2048,2048]{2,1,0:T(8,128)(2,1)} fusion(bf16[2,2048,2048]{2,1,0:T(8,128)(2,1)} %param.8, bf16[2048,2048]{1,0:T(8,128)(2,1)S(1)} %convolution_convert_fusion), kind=kLoop, calls=%fused_computation.7 | loop fusion | flops 8388608 | bytes 41943040 | tf_op jit(solution)/shard_map/mul | solution.py:52
  36.8 28.5 %all-gather.3.cloned.1.call-done = bf16[8192,256]{1,0:T(8,128)(2,1)} async-done(((bf16[2048,256]{1,0:T(8,128)(2,1)}), bf16[8192,256]{1,0:T(8,128)(2,1)}) %all-gather.3.cloned.1.call-update) | async-done | bytes 4194320 | tf_op jit(solution)/shard_map/all_gather | solution.py:44
  65.3 12.5 %fusion.3 = f32[2,2048,256]{2,1,0:T(8,128)} fusion(bf16[2,2048,2048]{2,1,0:T(8,128)(2,1)} %broadcast_multiply_fusion, bf16[8192,256]{1,0:T(8,128)(2,1)} %all-gather.3.cloned.1.call-done, s32[]{:T(128)S(6)} %select_n.32), kind=kOutput, calls=%fused_computation.11 | convolution fusion | flops 4294967296 | bytes 22020100 | tf_op jit(solution)/shard_map/pmn,ni->pmi/dot_general | solution.py:53
  77.8 147.4 %all-reduce.5 = bf16[2,2048,256]{2,1,0:T(8,128)(2,1)} all-reduce(f32[2,2048,256]{2,1,0:T(8,128)} %fusion.3), channel_id=1, replica_groups=mesh['grp'=2,'aux'=4,'orb'=4] {'orb'}, use_global_device_ids=true, to_apply=%region_0.1 | all-reduce | flops 1048576 | bytes 6291456 | tf_op jit(solution)/shard_map/psum | solution.py:54
  225.2 2.1 multiply_reduce_fusion.2
  227.3 73.3 %all-reduce = (bf16[2]{0:T(256)(128)(2,1)S(1)}, f32[64,128]{1,0:T(8,128)S(1)}) all-reduce(f32[2]{0:T(128)S(1)} %broadcast_multiply_fusion.1, f32[64,128]{1,0:T(8,128)S(1)} %fusion.29), channel_id=1, replica_groups=mesh['grp'=2,'aux'=4,'orb'=4] {'aux','orb'}, use_global_device_ids=true, to_apply=%region_1.2 | all-reduce | flops 8194 | bytes 65548 | tf_op jit(solution)/shard_map/psum | solution.py:59
  300.6 28.8 %fusion.1 = f32[1,2048,2048]{2,0,1:T(1,128)S(1)} fusion(bf16[2,2048,2048]{2,1,0:T(8,128)(2,1)} %broadcast_multiply_fusion, bf16[2]{0:T(256)(128)(2,1)S(1)} %get-tuple-element.2), kind=kOutput, calls=%fused_computation.4 | convolution fusion | flops 16777216 | bytes 33554436 | tf_op jit(solution)/shard_map/pmn,p->mn/dot_general | solution.py:60
  329.3 11.3 %copy.18 = f32[1,2048,2048]{2,1,0:T(8,128)} copy(f32[1,2048,2048]{2,0,1:T(1,128)S(1)} %fusion.1) | data formatting | bytes 33554432 | tf_op jit(solution)/shard_map/pmn,p->mn/dot_general | solution.py:60
  340.7 7.0 all-to-all-start
  347.6 0.0 all-gather.5.cloned.1.call-start
  347.7 0.7 all-gather.5.cloned.1.call-update
  348.4 0.0 all-reduce.4.cloned.1.call-start
  348.4 426.2 %all-to-all-done = f32[4,512,2048]{2,1,0:T(8,128)} async-done(((f32[4,512,2048]{2,1,0:T(8,128)}), f32[4,512,2048]{2,1,0:T(8,128)}, u32[]{:S(2)}, u32[]{:S(2)}) %all-to-all-start) | async-done | bytes 16777248 | tf_op jit(solution)/shard_map/all_to_all | solution.py:61
  774.6 11.9 %copy.21 = f32[4,64,8,2048]{3,2,0,1:T(8,128)} copy(f32[4,64,8,2048]{3,2,1,0:T(8,128)} %bitcast.23) | data formatting | bytes 33554432 | tf_op jit(solution)/shard_map/all_to_all | solution.py:61
  786.5 14.4 %fusion = f32[512,8192]{1,0:T(8,128)} fusion(f32[512,8192]{1,0:T(8,128)} %bitcast.58, bf16[2,512,256]{2,1,0:T(8,128)(2,1)S(1)} %copy-done.2, bf16[2,8192,256]{2,1,0:T(8,128)(2,1)} %all-gather.5.cloned.1.call-done), kind=kOutput, calls=%fused_computation.1 | convolution fusion | flops 4303355904 | bytes 42467328 | tf_op jit(solution)/shard_map/pmi,pni->mn/dot_general | solution.py:79
  800.9 0.0 all-reduce.4.cloned.1.call-update
  800.9 3.4 psum.39
  804.3 0.1 dynamic_slice.15
  804.4 3.9 multiply_reduce_fusion
  808.4 0.2 fusion.15
  808.6 1.3 fusion.7
  809.8 49.1 %all-reduce.4.cloned.1.call-done = f32[512,8192]{1,0:T(8,128)} async-done(((f32[512,8192]{1,0:T(8,128)}), f32[512,8192]{1,0:T(8,128)}) %all-reduce.4.cloned.1.call-update) | async-done | bytes 16777232 | tf_op jit(solution)/shard_map/psum | solution.py:86
  859.0 12.1 %select_add_fusion = f32[512,8192]{1,0:T(8,128)} fusion(f32[512,8192]{1,0:T(8,128)} %all-reduce.4.cloned.1.call-done, f32[512]{0:T(512)S(1)} %dynamic_slice.15, s32[512]{0:T(512)S(1)} %iota_add_fusion.2), kind=kLoop, calls=%fused_computation.2 | loop fusion | flops 12582912 | bytes 33558528 | tf_op jit(solution)/shard_map/add | solution.py:25
  (16 shorter events, 0.1 us)
Async XLA Ops:
  7.2 4.1 copy-start
  7.2 58.1 %all-gather.3.cloned.1.call-start = ((), (), s32[]{:S(2)}) async-start(), calls=%async_computation.1 | async-start | bytes 5242880 | tf_op jit(solution)/shard_map/all_gather | solution.py:44
  340.7 434.0 %all-to-all-start = ((f32[4,512,2048]{2,1,0:T(8,128)}), f32[4,512,2048]{2,1,0:T(8,128)}, u32[]{:S(2)}, u32[]{:S(2)}) async-start(f32[4,512,2048]{2,1,0:T(8,128)} %bitcast.57), calls=%async_computation | async-start | bytes 33554432 | tf_op jit(solution)/shard_map/all_to_all | solution.py:61
  347.6 438.9 %all-gather.5.cloned.1.call-start = ((), (), s32[]{:S(2)}) async-start(), calls=%async_computation.2 | async-start | bytes 8912896 | tf_op jit(solution)/shard_map/all_gather | solution.py:82
  348.4 510.6 %all-reduce.4.cloned.1.call-start = ((), (), s32[]{:S(2)}) async-start(), calls=%async_computation.3 | async-start | bytes 33554432 | tf_op jit(solution)/shard_map/psum | solution.py:86
  774.6 11.9 %copy-start.2 = (bf16[2,512,256]{2,1,0:T(8,128)(2,1)S(1)}, bf16[2,512,256]{2,1,0:T(8,128)(2,1)}, u32[]{:S(2)}) copy-start(bf16[2,512,256]{2,1,0:T(8,128)(2,1)} %get-tuple-element.5) | copy-start | bytes 1572868
  800.9 7.5 copy-start.3
  800.9 7.5 copy-start.4
  808.6 62.5 %copy-start.1 = (f32[1024]{0:T(1024)S(1)}, f32[1024]{0:T(1024)}, u32[]{:S(2)}) copy-start(f32[1024]{0:T(1024)} %param.14) | copy-start | bytes 12292
Sparse Core Ops, SparseCore 0:
  9.9 55.3 all-gather.2
  351.3 367.7 all-gather.4
  801.0 57.8 all-reduce.3
